TPU v7x, 256 devices: a whole 4x4x8 slice. The times are simulated.
256 devices in a mesh: dp: 32 (over x, z), tensor: 8 (over y, core).
Axes of the slice: x: 4, y: 4, z: 8, core: 2. Of those that a mesh axis runs over, the one named last changes fastest.
Arguments:
- tokens: bfloat16 [1024, 6144], P('dp', 'tensor'), may hold values from -32 to 32
- gain_in: float32 [6144], P('tensor'), may hold values from 0.1 to 1.9
- shift_in: float32 [6144], P('tensor'), may hold values from -3 to 3
- up_weight: bfloat16 [6144, 24576], P('tensor', 'dp'), may hold values from -0.078125 to 0.078125
- up_bias: float32 [24576], P('dp'), may hold values from -3 to 3
- down_weight: bfloat16 [24576, 6144], P('dp', 'tensor'), may hold values from -1 to 1
- gain_out: float32 [6144], P('tensor'), may hold values from 0.1 to 1.9
- curvature: float32 [1024, 6144], P('dp', 'tensor'), may hold values from 0.5 to 12
- up_tangent: bfloat16 [6144, 24576], P('tensor', 'dp'), may hold values from -0.078125 to 0.078125
- down_tangent: bfloat16 [24576, 6144], P('dp', 'tensor'), may hold values from -1 to 1
Outputs:
- up_product: float32 [6144, 24576], P('tensor', 'dp')
- down_product: float32 [24576, 6144], P('dp', 'tensor')
All inputs are finite; a program needn't handle non-finite values.
Results may differ from a plain program's by a relative error of at most 0.003.
Values may be sent and summed in bfloat16 or wider, within the bound.
A program may use at most 128 MiB of HBM per device.

v0:
```python
import jax
import jax.numpy as jnp
from jax import lax
from jax.sharding import PartitionSpec as P

D = 6144
epsilon = 1e-05
root_half = 0.7071067811865476
inv_root_two_pi = 0.3989422804014327


def gelu_value(values):
    return 0.5 * values * (1.0 + lax.erf(values * root_half))


def gelu_slope(values):
    return (
        0.5 * (1.0 + lax.erf(values * root_half))
        + values * jnp.exp(-0.5 * values * values) * inv_root_two_pi
    )


def row_total(values):
    return jnp.sum(values, axis=1)


def on_device(
    tokens,
    gain_in,
    shift_in,
    up_weight,
    up_bias,
    down_weight,
    gain_out,
    curvature,
    up_tangent,
    down_tangent,
):
    model_width = float(D)
    source = tokens.astype(jnp.float32)
    sum_in, square_in = lax.psum((row_total(source), row_total(source * source)), "tensor")
    center_in = sum_in / model_width
    spread_in = square_in / model_width - center_in * center_in
    inverse_in = lax.rsqrt(spread_in + epsilon)[:, None]
    normed = ((source - center_in[:, None]) * inverse_in * gain_in + shift_in).astype(jnp.bfloat16)
    all_normed = lax.all_gather(normed, "dp", axis=0, tiled=True)
    pre_part = jnp.dot(all_normed, up_weight, preferred_element_type=jnp.float32)
    tangent_part = jnp.dot(all_normed, up_tangent, preferred_element_type=jnp.float32)
    share_rows = all_normed.shape[0] // lax.axis_size("tensor")
    pre_total, tangent_total = lax.psum((pre_part, tangent_part), "tensor")
    pre_full = pre_total + up_bias
    slope_full = gelu_slope(pre_full)
    hidden = gelu_value(pre_full).astype(jnp.bfloat16)
    hidden_tangent = (slope_full * tangent_total).astype(jnp.bfloat16)
    slope_rows = lax.dynamic_slice_in_dim(
        slope_full, lax.axis_index("tensor") * share_rows, share_rows, 0
    )
    slope_kept = lax.optimization_barrier(slope_rows.astype(jnp.bfloat16))
    primal = jnp.dot(hidden, down_weight, preferred_element_type=jnp.float32)
    tangent = jnp.dot(hidden_tangent, down_weight, preferred_element_type=jnp.float32) + jnp.dot(
        hidden, down_tangent, preferred_element_type=jnp.float32
    )
    both_outputs = lax.psum_scatter(
        jnp.concatenate([primal, tangent], axis=1), "dp", scatter_dimension=0, tiled=True
    )
    local_width = down_weight.shape[1]
    output = source + both_outputs[:, :local_width]
    output_tangent = both_outputs[:, local_width:]
    factor = gain_out * gain_out * curvature
    sum_out, square_out = lax.psum((row_total(output), row_total(output * output)), "tensor")
    center_out = sum_out / model_width
    inverse_out = lax.rsqrt(square_out / model_width - center_out * center_out + epsilon)[:, None]
    normal_out = (output - center_out[:, None]) * inverse_out
    tangent_sum, tangent_dot = lax.psum(
        (row_total(output_tangent), row_total(normal_out * output_tangent)), "tensor"
    )
    normal_tangent = (
        output_tangent
        - (tangent_sum / model_width)[:, None]
        - normal_out * (tangent_dot / model_width)[:, None]
    ) * inverse_out
    weighted = factor * normal_tangent
    weight_sum, weight_dot = lax.psum(
        (row_total(weighted), row_total(normal_out * weighted)), "tensor"
    )
    cotangent = (
        (
            weighted
            - (weight_sum / model_width)[:, None]
            - normal_out * (weight_dot / model_width)[:, None]
        )
        * inverse_out
    ).astype(jnp.bfloat16)
    all_cotangent = lax.all_gather(cotangent, "dp", axis=0, tiled=True)
    back_part = lax.dot_general(
        all_cotangent, down_weight, (((1,), (1,)), ((), ())), preferred_element_type=jnp.float32
    )
    down_product = lax.dot_general(
        hidden, all_cotangent, (((0,), (0,)), ((), ())), preferred_element_type=jnp.float32
    )
    back_share = lax.psum_scatter(back_part, "tensor", scatter_dimension=0, tiled=True)
    grad_share = (back_share * slope_kept.astype(jnp.float32)).astype(jnp.bfloat16)
    grad_pre = lax.all_gather(grad_share, "tensor", axis=0, tiled=True)
    up_product = lax.dot_general(
        all_normed, grad_pre, (((0,), (0,)), ((), ())), preferred_element_type=jnp.float32
    )
    return (up_product, down_product)


def solution(mesh):
    return jax.shard_map(
        on_device,
        mesh=mesh,
        in_specs=(
            P("dp", "tensor"),
            P("tensor"),
            P("tensor"),
            P("tensor", "dp"),
            P("dp"),
            P("dp", "tensor"),
            P("tensor"),
            P("dp", "tensor"),
            P("tensor", "dp"),
            P("dp", "tensor"),
        ),
        out_specs=(P("tensor", "dp"), P("dp", "tensor")),
        check_vma=False,
    )
```

profile of v0, /device:TPU:1, one launch (start us, length us, event | category | flops | bytes accessed | tf_op | source)
XLA Modules:
  0.0 637.0 jit_solution(9508748308312653953)
XLA Ops:
  7.2 1.0 convert_reduce_fusion
  8.2 15.0 %all-reduce.3 = (f32[32]{0:T(128)S(1)}, f32[32]{0:T(128)S(1)}) all-reduce(f32[32]{0:T(128)S(1)} %get-tuple-element.9, f32[32]{0:T(128)S(1)} %get-tuple-element.8), channel_id=1, replica_groups=mesh['dp'=32,'tensor'=8] {'tensor'}, use_global_device_ids=true, to_apply=%region_3.0 | all-reduce | flops 64 | bytes 512 | tf_op jit(solution)/shard_map/psum | solution.py:41
  23.3 1.5 fusion.8
  24.9 74.0 %all-gather.4.cloned.1.call-done = bf16[1024,768]{1,0:T(8,128)(2,1)} async-done(((bf16[32,768]{1,0:T(8,128)(2,1)}), bf16[1024,768]{1,0:T(8,128)(2,1)}) %all-gather.4.cloned.1.call-update) | async-done | bytes 1572880 | tf_op jit(solution)/shard_map/all_gather | solution.py:46
  98.8 4.9 fusion.14
  103.7 4.4 fusion.12
  108.1 91.1 %all-reduce.7.cloned.1.call-done = (f32[1024,768]{1,0:T(8,128)}, f32[1024,768]{1,0:T(8,128)}) async-done(((f32[1024,768]{1,0:T(8,128)}, f32[1024,768]{1,0:T(8,128)}), (f32[1024,768]{1,0:T(8,128)}, f32[1024,768]{1,0:T(8,128)})) %all-reduce.7.cloned.1.call-update) | async-done | bytes 6291472 | tf_op jit(solution)/shard_map/psum | solution.py:50
  199.2 3.0 multiply_convert_fusion.1
  202.2 1.4 fusion.13
  203.9 1.4 copy-done.2
  205.2 1.4 fusion.4
  206.7 1.4 convolution_add_fusion
  208.1 3.2 pad_maximum_fusion
  211.4 6.6 %copy.16 = f32[1024,1536]{1,0:T(8,128)} copy(f32[1024,1536]{0,1:T(8,128)} %pad_maximum_fusion) | data formatting | bytes 12582912
  218.1 0.6 copy-done.6
  218.7 218.9 %reduce-scatter.7.cloned.1.call-done = f32[32,1536]{1,0:T(8,128)} async-done(((f32[1024,1536]{1,0:T(8,128)}), f32[32,1536]{1,0:T(8,128)}) %reduce-scatter.7.cloned.1.call-update) | async-done | bytes 196624 | tf_op jit(solution)/shard_map/reduce_scatter | solution.py:63
  437.6 1.0 fusion.11
  438.6 16.9 %all-reduce.2 = (f32[32]{0:T(128)S(1)}, f32[32]{0:T(128)S(1)}) all-reduce(f32[32]{0:T(128)S(1)} %get-tuple-element.7, f32[32]{0:T(128)S(1)} %get-tuple-element.6), channel_id=1, replica_groups=mesh['dp'=32,'tensor'=8] {'tensor'}, use_global_device_ids=true, to_apply=%region_12.0 | all-reduce | flops 64 | bytes 512 | tf_op jit(solution)/shard_map/psum | solution.py:70
  455.5 1.1 slice_reduce_fusion
  456.6 12.4 %all-reduce.1 = (f32[32]{0:T(128)S(1)}, f32[32]{0:T(128)S(1)}) all-reduce(f32[32]{0:T(128)S(1)} %get-tuple-element.3, f32[32]{0:T(128)S(1)} %get-tuple-element.2), channel_id=1, replica_groups=mesh['dp'=32,'tensor'=8] {'tensor'}, use_global_device_ids=true, to_apply=%region_14.0 | all-reduce | flops 64 | bytes 512 | tf_op jit(solution)/shard_map/psum | solution.py:74
  469.0 1.1 fusion.10
  470.1 12.4 %all-reduce = (f32[32]{0:T(128)S(1)}, f32[32]{0:T(128)S(1)}) all-reduce(f32[32]{0:T(128)S(1)} %get-tuple-element.5, f32[32]{0:T(128)S(1)} %get-tuple-element.4), channel_id=1, replica_groups=mesh['dp'=32,'tensor'=8] {'tensor'}, use_global_device_ids=true, to_apply=%region_18.0 | all-reduce | flops 64 | bytes 512 | tf_op jit(solution)/shard_map/psum | solution.py:83
  482.6 0.7 multiply_convert_fusion.4
  483.3 68.7 %all-gather.6.cloned.1.call-done = bf16[1024,768]{1,0:T(8,128)(2,1)} async-done(((bf16[32,768]{1,0:T(8,128)(2,1)}), bf16[1024,768]{1,0:T(8,128)(2,1)}) %all-gather.6.cloned.1.call-update) | async-done | bytes 1572880 | tf_op jit(solution)/shard_map/all_gather | solution.py:94
  552.1 4.5 fusion.15
  556.6 0.2 all-gather.8.cloned.1.call-start
  556.8 1.0 dynamic-slice_convert_fusion
  557.9 36.3 %reduce-scatter.5.cloned.1.call-done = f32[128,768]{1,0:T(8,128)} async-done(((f32[1024,768]{1,0:T(8,128)}), f32[128,768]{1,0:T(8,128)}) %reduce-scatter.5.cloned.1.call-update) | async-done | bytes 393232 | tf_op jit(solution)/shard_map/reduce_scatter | solution.py:101
  594.1 1.7 multiply_convert_fusion.3
  595.9 4.3 fusion.17
  600.1 25.4 %all-gather.8.cloned.1.call-done = bf16[1024,768]{1,0:T(8,128)(2,1)} async-done(((bf16[128,768]{1,0:T(8,128)(2,1)}), bf16[1024,768]{1,0:T(8,128)(2,1)}) %all-gather.8.cloned.1.call-update) | async-done | bytes 1572880 | tf_op jit(solution)/shard_map/all_gather | solution.py:103
  625.5 4.7 fusion.16
  (33 shorter events, 0.6 us)
Async XLA Ops:
  7.2 195.0 %copy-start = (bf16[768,768]{1,0:T(8,128)(2,1)S(1)}, bf16[768,768]{1,0:T(8,128)(2,1)}, u32[]{:S(2)}) copy-start(bf16[768,768]{1,0:T(8,128)(2,1)} %param.15) | copy-start | bytes 3538948
  7.2 91.7 %all-gather.4.cloned.1.call-start = ((), (), s32[]{:S(2)}) async-start(), calls=%async_computation.2 | async-start | bytes 1622016 | tf_op jit(solution)/shard_map/all_gather | solution.py:46
  24.8 174.4 %all-reduce.7.cloned.1.call-start = ((), (), s32[]{:S(2)}) async-start(), calls=%async_computation.7 | async-start | bytes 12582912 | tf_op jit(solution)/shard_map/psum | solution.py:50
  98.8 4.9 copy-start.8
  108.1 91.1 %copy-start.7 = (f32[768]{0:T(1024)S(1)}, f32[768]{0:T(1024)}, u32[]{:S(2)}) copy-start(f32[768]{0:T(1024)} %param.14) | copy-start | bytes 9220
  108.1 329.5 %reduce-scatter.7.cloned.1.call-start = ((), (), s32[]{:S(2)}) async-start(), calls=%async_computation.6 | async-start | bytes 6488064 | tf_op jit(solution)/shard_map/reduce_scatter | solution.py:63
  202.2 1.7 copy-start.1
  202.2 3.0 copy-start.2
  205.2 1.4 copy-start.3
  218.0 0.7 copy-start.6
  218.0 219.6 %copy-start.4 = (bf16[32,768]{1,0:T(8,128)(2,1)S(1)}, bf16[32,768]{1,0:T(8,128)(2,1)}, u32[]{:S(2)}) copy-start(bf16[32,768]{1,0:T(8,128)(2,1)} %param.10) | copy-start | bytes 147460
  218.0 251.0 %copy-start.5 = (f32[32,768]{1,0:T(8,128)S(1)}, f32[32,768]{1,0:T(8,128)}, u32[]{:S(2)}) copy-start(f32[32,768]{1,0:T(8,128)} %param.17) | copy-start | bytes 294916
  218.0 334.1 %all-gather.6.cloned.1.call-start = ((), (), s32[]{:S(2)}) async-start(), calls=%async_computation.3 | async-start | bytes 1622016 | tf_op jit(solution)/shard_map/all_gather | solution.py:94
  483.3 110.8 %reduce-scatter.5.cloned.1.call-start = ((), (), s32[]{:S(2)}) async-start(), calls=%async_computation.4 | async-start | bytes 3538944 | tf_op jit(solution)/shard_map/reduce_scatter | solution.py:101
  556.6 68.9 %all-gather.8.cloned.1.call-start = ((), (), s32[]{:S(2)}) async-start(), calls=%async_computation.5 | async-start | bytes 1769472 | tf_op jit(solution)/shard_map/all_gather | solution.py:103
Sparse Core Ops, SparseCore 0:
  24.9 73.8 all-gather.3
  108.2 90.9 all-reduce.6
  218.1 219.3 reduce-scatter.6
  483.4 68.6 all-gather.5
  556.7 37.3 reduce-scatter.4
  596.5 28.8 all-gather.7
where the time goes:
time: 638 us; the launch traced here: 637 us
  waiting for transfers between devices  514 us (81%)
  blocking collectives  56.8 us (9%)
  matrix products  27 us (4%)
  other arithmetic  14.4 us (2%)
  between operations  14.2 us (2%)
  local copies, waits for them, and re-layouts  9.84 us (2%)
    reduce_scatter x1, waiting for transfers between devices, on_device(): lax.psum_scatter(jnp.concatenate([primal, tangent], axis=1), 'dp', scatte...  219 us
    psum x1, waiting for transfers between devices, on_device(): pre_total, tangent_total = lax.psum((pre_part, tangent_part), 'tensor')  91.1 us
    all_gather x1, waiting for transfers between devices, on_device(): all_normed = lax.all_gather(normed, 'dp', axis=0, tiled=True)  74 us
    all_gather x1, waiting for transfers between devices, on_device(): all_cotangent = lax.all_gather(cotangent, 'dp', axis=0, tiled=True)  68.7 us
    reduce_scatter x1, waiting for transfers between devices, on_device(): lax.psum_scatter(back_part, 'tensor', scatter_dimension=0, tiled=True)  36.3 us
    all_gather x1, waiting for transfers between devices, on_device(): grad_pre = lax.all_gather(grad_share, 'tensor', axis=0, tiled=True)  25.4 us
    psum x1, blocking collectives, on_device(): lax.psum((row_total(output), row_total(output * output)), 'tensor')  16.9 us
    psum x1, blocking collectives, on_device(): lax.psum((row_total(source), row_total(source * source)), 'tensor')  15 us
  transfers between devices with their start and end apart: 6, of which 6 were waited for; matrix products, arithmetic and copies ran while one was open for 1% of the time, Pallas kernels for 0%

commit v1 on v0

--- a/solution.py
+++ b/solution.py
@@ -43,7 +43,15 @@
     spread_in = square_in / model_width - center_in * center_in
     inverse_in = lax.rsqrt(spread_in + epsilon)[:, None]
     normed = ((source - center_in[:, None]) * inverse_in * gain_in + shift_in).astype(jnp.bfloat16)
-    all_normed = lax.all_gather(normed, "dp", axis=0, tiled=True)
+    all_normed = jnp.concatenate(
+        lax.all_to_all(
+            jnp.stack([normed for _ in range(lax.axis_size("dp"))]),
+            axis_name="dp",
+            split_axis=0,
+            concat_axis=0,
+        ),
+        axis=0,
+    )
     pre_part = jnp.dot(all_normed, up_weight, preferred_element_type=jnp.float32)
     tangent_part = jnp.dot(all_normed, up_tangent, preferred_element_type=jnp.float32)
     share_rows = all_normed.shape[0] // lax.axis_size("tensor")

time: 638 us -> 603 us (0.945)
  waiting for transfers between devices: 514 us -> 441 us
  blocking collectives: 56.8 us -> 100 us
    all_gather x1 -> x0, waiting for transfers between devices: 74 us -> none  [on_device(): all_normed = lax.all_gather(normed, 'dp', axis=0, tiled=True)]
    all_to_all x0 -> x1, blocking collectives: none -> 43.9 us  [on_device(): lax.all_to_all(jnp.stack([normed for _ in range(lax.axis_size('dp'))]), a...]
  transfers between devices with their start and end apart: 6 -> 5, of which waited for: 6 -> 5; matrix products, arithmetic and copies ran while one was open for 1% -> 1% of each run, Pallas kernels for 0% -> 0%
where the time goes in v1:
time: 603 us
  waiting for transfers between devices  441 us (73%)
  blocking collectives  100 us (17%)
  matrix products  23.9 us (4%)
  between operations  13.9 us (2%)
  other arithmetic  13.8 us (2%)
  local copies, waits for them, and re-layouts  10 us (2%)
    reduce_scatter x1, waiting for transfers between devices, on_device(): lax.psum_scatter(jnp.concatenate([primal, tangent], axis=1), 'dp', scatte...  219 us
    psum x1, waiting for transfers between devices, on_device(): pre_total, tangent_total = lax.psum((pre_part, tangent_part), 'tensor')  90.8 us
    all_gather x1, waiting for transfers between devices, on_device(): all_cotangent = lax.all_gather(cotangent, 'dp', axis=0, tiled=True)  68.7 us
    all_to_all x1, blocking collectives, on_device(): lax.all_to_all(jnp.stack([normed for _ in range(lax.axis_size('dp'))]), a...  43.9 us
    reduce_scatter x1, waiting for transfers between devices, on_device(): lax.psum_scatter(back_part, 'tensor', scatter_dimension=0, tiled=True)  36.3 us
    all_gather x1, waiting for transfers between devices, on_device(): grad_pre = lax.all_gather(grad_share, 'tensor', axis=0, tiled=True)  25.4 us
    psum x1, blocking collectives, on_device(): lax.psum((row_total(output), row_total(output * output)), 'tensor')  16.4 us
    psum x1, blocking collectives, on_device(): lax.psum((row_total(source), row_total(source * source)), 'tensor')  15 us
  transfers between devices with their start and end apart: 5, of which 5 were waited for; matrix products, arithmetic and copies ran while one was open for 1% of the time, Pallas kernels for 0%

profile of v1, /device:TPU:1, one launch (start us, length us, event | category | flops | bytes accessed | tf_op | source)
XLA Modules:
  0.0 602.7 jit_solution(5891099124813608627)
XLA Ops:
  7.2 1.0 convert_reduce_fusion
  8.2 15.0 %all-reduce.3 = (f32[32]{0:T(128)S(1)}, f32[32]{0:T(128)S(1)}) all-reduce(f32[32]{0:T(128)S(1)} %get-tuple-element.9, f32[32]{0:T(128)S(1)} %get-tuple-element.8), channel_id=1, replica_groups=mesh['dp'=32,'tensor'=8] {'tensor'}, use_global_device_ids=true, to_apply=%region_3.0 | all-reduce | flops 64 | bytes 512 | tf_op jit(solution)/shard_map/psum | solution.py:41
  23.3 0.9 fusion.8
  24.4 43.9 %all_to_all.5 = bf16[32,32,768]{2,1,0:T(8,128)(2,1)S(1)} all-to-all(bf16[32,32,768]{2,1,0:T(8,128)(2,1)S(1)} %stack.2), channel_id=1, replica_groups=mesh['dp'=32,'tensor'=8] {'dp'}, dimensions={0} | all-to-all | bytes 3145728 | tf_op jit(solution)/shard_map/all_to_all | solution.py:47
  68.3 3.0 fusion.14
  71.3 3.1 fusion.12
  74.5 90.8 %all-reduce.7.cloned.1.call-done = (f32[1024,768]{1,0:T(8,128)}, f32[1024,768]{1,0:T(8,128)}) async-done(((f32[1024,768]{1,0:T(8,128)}, f32[1024,768]{1,0:T(8,128)}), (f32[1024,768]{1,0:T(8,128)}, f32[1024,768]{1,0:T(8,128)})) %all-reduce.7.cloned.1.call-update) | async-done | bytes 6291472 | tf_op jit(solution)/shard_map/psum | solution.py:58
  165.3 3.0 multiply_convert_fusion.1
  168.3 1.4 fusion.13
  169.9 1.4 copy-done.2
  171.3 1.4 fusion.4
  172.7 1.4 convolution_add_fusion
  174.2 3.2 pad_maximum_fusion
  177.4 6.6 %copy.21 = f32[1024,1536]{1,0:T(8,128)} copy(f32[1024,1536]{0,1:T(8,128)} %pad_maximum_fusion) | data formatting | bytes 12582912
  184.1 0.6 copy-done.7
  184.7 219.3 %reduce-scatter.7.cloned.1.call-done = f32[32,1536]{1,0:T(8,128)} async-done(((f32[1024,1536]{1,0:T(8,128)}), f32[32,1536]{1,0:T(8,128)}) %reduce-scatter.7.cloned.1.call-update) | async-done | bytes 196624 | tf_op jit(solution)/shard_map/reduce_scatter | solution.py:71
  404.1 1.0 fusion.11
  405.1 16.4 %all-reduce.2 = (f32[32]{0:T(128)S(1)}, f32[32]{0:T(128)S(1)}) all-reduce(f32[32]{0:T(128)S(1)} %get-tuple-element.7, f32[32]{0:T(128)S(1)} %get-tuple-element.6), channel_id=1, replica_groups=mesh['dp'=32,'tensor'=8] {'tensor'}, use_global_device_ids=true, to_apply=%region_12.0 | all-reduce | flops 64 | bytes 512 | tf_op jit(solution)/shard_map/psum | solution.py:78
  421.5 1.1 slice_reduce_fusion
  422.6 12.4 %all-reduce.1 = (f32[32]{0:T(128)S(1)}, f32[32]{0:T(128)S(1)}) all-reduce(f32[32]{0:T(128)S(1)} %get-tuple-element.3, f32[32]{0:T(128)S(1)} %get-tuple-element.2), channel_id=1, replica_groups=mesh['dp'=32,'tensor'=8] {'tensor'}, use_global_device_ids=true, to_apply=%region_14.0 | all-reduce | flops 64 | bytes 512 | tf_op jit(solution)/shard_map/psum | solution.py:82
  435.0 1.1 fusion.10
  436.1 12.4 %all-reduce = (f32[32]{0:T(128)S(1)}, f32[32]{0:T(128)S(1)}) all-reduce(f32[32]{0:T(128)S(1)} %get-tuple-element.5, f32[32]{0:T(128)S(1)} %get-tuple-element.4), channel_id=1, replica_groups=mesh['dp'=32,'tensor'=8] {'tensor'}, use_global_device_ids=true, to_apply=%region_18.0 | all-reduce | flops 64 | bytes 512 | tf_op jit(solution)/shard_map/psum | solution.py:91
  448.6 0.7 multiply_convert_fusion.4
  449.4 68.7 %all-gather.3.cloned.1.call-done = bf16[1024,768]{1,0:T(8,128)(2,1)} async-done(((bf16[32,768]{1,0:T(8,128)(2,1)}), bf16[1024,768]{1,0:T(8,128)(2,1)}) %all-gather.3.cloned.1.call-update) | async-done | bytes 1572880 | tf_op jit(solution)/shard_map/all_gather | solution.py:102
  518.1 4.5 fusion.15
  522.6 0.2 all-gather.5.cloned.1.call-start
  522.8 1.0 dynamic-slice_convert_fusion
  523.9 36.3 %reduce-scatter.5.cloned.1.call-done = f32[128,768]{1,0:T(8,128)} async-done(((f32[1024,768]{1,0:T(8,128)}), f32[128,768]{1,0:T(8,128)}) %reduce-scatter.5.cloned.1.call-update) | async-done | bytes 393232 | tf_op jit(solution)/shard_map/reduce_scatter | solution.py:109
  560.1 1.7 multiply_convert_fusion.3
  561.9 4.3 fusion.17
  566.1 25.4 %all-gather.5.cloned.1.call-done = bf16[1024,768]{1,0:T(8,128)(2,1)} async-done(((bf16[128,768]{1,0:T(8,128)(2,1)}), bf16[1024,768]{1,0:T(8,128)(2,1)}) %all-gather.5.cloned.1.call-update) | async-done | bytes 1572880 | tf_op jit(solution)/shard_map/all_gather | solution.py:111
  591.5 4.7 fusion.16
  (36 shorter events, 0.7 us)
Async XLA Ops:
  7.2 161.1 %copy-start = (bf16[768,768]{1,0:T(8,128)(2,1)S(1)}, bf16[768,768]{1,0:T(8,128)(2,1)}, u32[]{:S(2)}) copy-start(bf16[768,768]{1,0:T(8,128)(2,1)} %param.15) | copy-start | bytes 3538948
  7.2 158.1 %all-reduce.7.cloned.1.call-start = ((), (), s32[]{:S(2)}) async-start(), calls=%async_computation.7 | async-start | bytes 12582912 | tf_op jit(solution)/shard_map/psum | solution.py:58
  24.3 44.0 %copy-start.9 = (bf16[768,768]{1,0:T(8,128)(2,1)S(1)}, bf16[768,768]{1,0:T(8,128)(2,1)}, u32[]{:S(2)}) copy-start(bf16[768,768]{1,0:T(8,128)(2,1)} %param.18) | copy-start | bytes 3538948
  68.3 3.0 copy-start.3
  68.3 3.0 copy-start.10
  74.4 90.8 %copy-start.8 = (f32[768]{0:T(1024)S(1)}, f32[768]{0:T(1024)}, u32[]{:S(2)}) copy-start(f32[768]{0:T(1024)} %param.14) | copy-start | bytes 9220
  74.4 329.6 %reduce-scatter.7.cloned.1.call-start = ((), (), s32[]{:S(2)}) async-start(), calls=%async_computation.6 | async-start | bytes 6488064 | tf_op jit(solution)/shard_map/reduce_scatter | solution.py:71
  168.2 1.7 copy-start.1
  168.3 3.0 copy-start.2
  171.3 1.4 copy-start.4
  184.0 0.7 copy-start.7
  184.0 220.0 %copy-start.5 = (bf16[32,768]{1,0:T(8,128)(2,1)S(1)}, bf16[32,768]{1,0:T(8,128)(2,1)}, u32[]{:S(2)}) copy-start(bf16[32,768]{1,0:T(8,128)(2,1)} %param.10) | copy-start | bytes 147460
  184.0 251.0 %copy-start.6 = (f32[32,768]{1,0:T(8,128)S(1)}, f32[32,768]{1,0:T(8,128)}, u32[]{:S(2)}) copy-start(f32[32,768]{1,0:T(8,128)} %param.17) | copy-start | bytes 294916
  184.0 334.0 %all-gather.3.cloned.1.call-start = ((), (), s32[]{:S(2)}) async-start(), calls=%async_computation.3 | async-start | bytes 1622016 | tf_op jit(solution)/shard_map/all_gather | solution.py:102
  449.3 110.8 %reduce-scatter.5.cloned.1.call-start = ((), (), s32[]{:S(2)}) async-start(), calls=%async_computation.4 | async-start | bytes 3538944 | tf_op jit(solution)/shard_map/reduce_scatter | solution.py:109
  522.6 68.9 %all-gather.5.cloned.1.call-start = ((), (), s32[]{:S(2)}) async-start(), calls=%async_computation.5 | async-start | bytes 1769472 | tf_op jit(solution)/shard_map/all_gather | solution.py:111
Sparse Core Ops, SparseCore 0:
  74.6 90.6 all-reduce.6
  184.2 219.8 reduce-scatter.6
  449.4 68.6 all-gather.2
  522.7 37.3 reduce-scatter.4
  562.5 28.8 all-gather.4
